TPU v7x, 32 devices: a whole 2x2x4 slice. The times are simulated.
32 devices in a mesh: tm: 16 (over z, x, core), fsdp: 2 (over y).
Axes of the slice: x: 2, y: 2, z: 4, core: 2. Of those that a mesh axis runs over, the one named last changes fastest.
Arguments:
- frames: bfloat16 [2, 2, 24576, 512], P(None, 'fsdp', 'tm'), may hold values from -6 to 6
- conditioning: bfloat16 [2, 2, 24576, 512], P(None, 'fsdp', 'tm'), may hold values from -6 to 6
- lengths: int32 [2, 2, 30], P(None, 'fsdp'), may hold values from 1 to 1600, 24576 in all within a row
- steps: int32 [2, 2, 30], P(None, 'fsdp'), may hold values from 0 to 999
- prompt: bfloat16 [2, 2, 256, 512], P(None, 'fsdp', 'tm'), may hold values from -6 to 6
- queries: float32 [32, 512], P('fsdp'), may hold values from -6 to 6
- w_step: float32 [512, 1024], P('fsdp'), may hold values from -0.25 to 0.25
- w_cond: float32 [512, 1024], P('fsdp'), may hold values from -0.25 to 0.25
- w_conv: float32 [3, 512, 1024], P(None, 'fsdp'), may hold values from -0.15625 to 0.15625
- w_query: float32 [512, 512], P('fsdp'), may hold values from -0.25 to 0.25
- w_key: float32 [512, 512], P('fsdp'), may hold values from -0.25 to 0.25
- w_value: float32 [512, 512], P('fsdp'), may hold values from -0.25 to 0.25
- w_out: float32 [512, 512], P('fsdp'), may hold values from -2 to 2
- w_film: float32 [512, 1024], P('fsdp'), may hold values from -2 to 2
- w_proj: float32 [512, 1024], P('fsdp'), may hold values from -0.25 to 0.25
- grad_res: bfloat16 [2, 2, 24576, 512], P(None, 'fsdp', 'tm'), may hold values from -6 to 6
- grad_skip: bfloat16 [2, 2, 24576, 512], P(None, 'fsdp', 'tm'), may hold values from -6 to 6
Outputs:
- res_out: bfloat16 [2, 2, 24576, 512], P(None, 'fsdp', 'tm')
- skip_out: bfloat16 [2, 2, 24576, 512], P(None, 'fsdp', 'tm')
- grad_frames: float32 [2, 2, 24576, 512], P(None, 'fsdp', 'tm')
- grad_prompt: float32 [2, 2, 256, 512], P(None, 'fsdp', 'tm')
- grad_queries: float32 [32, 512], P('fsdp')
- grad_step: float32 [512, 1024], P('fsdp')
- grad_cond: float32 [512, 1024], P('fsdp')
- grad_conv: float32 [3, 512, 1024], P(None, 'fsdp')
- grad_query: float32 [512, 512], P('fsdp')
- grad_key: float32 [512, 512], P('fsdp')
- grad_value: float32 [512, 512], P('fsdp')
- grad_out: float32 [512, 512], P('fsdp')
- grad_film: float32 [512, 1024], P('fsdp')
- grad_proj: float32 [512, 1024], P('fsdp')
Inputs may be any that keep to these rules, and one draw needn't show every extreme that they name: Each pack's 30 lengths sum to its 24576 frames; the last entry is the padding at the pack's end; the longest entry is exactly 1600.
All inputs are finite; a program needn't handle non-finite values.
Results may differ from a plain program's by a relative error of at most 0.0085.
The roundings to bfloat16 on the way count: a program that leaves them out, or rounds other values in their place, can miss the bound.
Values may be sent and summed in bfloat16 or wider, within the bound.
No kernel may reach another device: no remote copies, remote signals or barrier semaphores. Data moves between devices by JAX's collectives and lax.ppermute only.
A program may use at most 104 MiB of HBM per device.

v0:
```python
import math
import jax
import jax.numpy as jnp
from jax import lax
from jax.sharding import PartitionSpec as P

HEADS = 8
QUERIES = 32
DILATION = 16
MICRO = 2
PRECISE = lax.Precision.HIGHEST
SQRT_HALF = 0.7071067811865476


def padded(block, sides, width):
    for axis, dim in sides:
        count = lax.axis_size(axis)
        forward = [(i, i + 1) for i in range(count - 1)]
        backward = [(target, source) for source, target in forward]
        low = lax.ppermute(
            lax.slice_in_dim(block, block.shape[dim] - width, None, axis=dim), axis, forward
        )
        high = lax.ppermute(lax.slice_in_dim(block, 0, width, axis=dim), axis, backward)
        block = jnp.concatenate([low, block, high], axis=dim)
    return block


def joined_2(part, axis, combine):
    gathered = jax.tree.map(lambda a: lax.all_gather(a, axis), part)

    def take(source):
        return jax.tree.map(lambda a: lax.dynamic_index_in_dim(a, source, 0, False), gathered)

    return lax.fori_loop(
        1, lax.axis_size(axis), lambda source, state: combine(state, take(source)), take(0)
    )


def contract_rows(left, right, precision=None):
    return lax.dot_general(
        left,
        right,
        (((0,), (0,)), ((), ())),
        precision=precision,
        preferred_element_type=jnp.float32,
    )


def contract_cols(left, right, precision=None):
    return lax.dot_general(
        left,
        right,
        (((1,), (1,)), ((), ())),
        precision=precision,
        preferred_element_type=jnp.float32,
    )


def softmax_join(earlier, later):
    joined = jnp.maximum(earlier[0], later[0])
    return (
        joined,
        earlier[1] * jnp.exp(earlier[0] - joined) + later[1] * jnp.exp(later[0] - joined),
    )


def step_embedding(pack_steps, width):
    half_width = width // 2
    freqs = jnp.exp(jnp.arange(half_width).astype(jnp.float32) * (-math.log(10000.0) / half_width))
    angles = pack_steps.astype(jnp.float32)[:, None] * freqs[None, :]
    return jnp.concatenate([jnp.sin(angles), jnp.cos(angles)], axis=1)


def per_device(
    frames,
    conditioning,
    lengths,
    steps,
    prompt,
    queries,
    w_step,
    w_cond,
    w_conv,
    w_query,
    w_key,
    w_value,
    w_out,
    w_film,
    w_proj,
    grad_res,
    grad_skip,
):
    frames_dev = frames.shape[2]
    width = frames.shape[3]
    prompt_rows_dev = prompt.shape[2]
    head_size = width // HEADS
    score_scale = 1.0 / math.sqrt(head_size)
    bf16 = jnp.bfloat16
    f32 = jnp.float32
    shard_q = queries.astype(bf16)
    shard_step = w_step.astype(bf16)
    shard_cond = w_cond.astype(bf16)
    shard_conv = w_conv.astype(bf16)
    shard_query = w_query.astype(bf16)
    shard_key = w_key.astype(bf16)
    shard_value = w_value.astype(bf16)
    shard_out = w_out.astype(bf16)
    shard_film = w_film.astype(bf16)
    shard_proj = w_proj.astype(bf16)
    tm_index = lax.axis_index("tm")
    first_rank = (tm_index == 0).astype(f32)
    acc_q = jnp.zeros((QUERIES, width), f32)
    acc_step = jnp.zeros((width, 2 * width), f32)
    acc_cond = jnp.zeros((width, 2 * width), f32)
    acc_conv = jnp.zeros((3 * width, 2 * width), f32)
    acc_query = jnp.zeros((width, width), f32)
    acc_key = jnp.zeros((width, width), f32)
    acc_value = jnp.zeros((width, width), f32)
    acc_out = jnp.zeros((width, width), f32)
    acc_film = jnp.zeros((width, 2 * width), f32)
    acc_proj = jnp.zeros((width, 2 * width), f32)
    res_list, skip_list, frame_list, prompt_list = ([], [], [], [])
    for micro_index in range(MICRO):
        gathered = (
            lax.all_gather(shard_q, "fsdp", axis=0, tiled=True),
            lax.all_gather(shard_step, "fsdp", axis=0, tiled=True),
            lax.all_gather(shard_cond, "fsdp", axis=0, tiled=True),
            lax.all_gather(shard_conv, "fsdp", axis=1, tiled=True),
            lax.all_gather(shard_query, "fsdp", axis=0, tiled=True),
            lax.all_gather(shard_key, "fsdp", axis=0, tiled=True),
            lax.all_gather(shard_value, "fsdp", axis=0, tiled=True),
            lax.all_gather(shard_out, "fsdp", axis=0, tiled=True),
            lax.all_gather(shard_film, "fsdp", axis=0, tiled=True),
            lax.all_gather(shard_proj, "fsdp", axis=0, tiled=True),
        )
        (
            full_q,
            full_step,
            full_cond,
            full_conv,
            full_query,
            full_key,
            full_value,
            full_out,
            full_film,
            full_proj,
        ) = gathered
        conv_flat = full_conv.reshape(3 * width, 2 * width)
        frame_rows = frames[micro_index, 0].astype(f32)
        cond_rows = conditioning[micro_index, 0]
        pack_lengths = lengths[micro_index, 0]
        utter_count = pack_lengths.shape[0]
        utter_ends = jnp.cumsum(pack_lengths)
        positions = tm_index * frames_dev - DILATION + jnp.arange(frames_dev + 2 * DILATION)
        seg_ext = jnp.sum((positions[:, None] >= utter_ends[None, :]).astype(jnp.int32), axis=1)
        segment = seg_ext[DILATION : DILATION + frames_dev]
        live_mask = (segment < utter_count - 1).astype(f32)
        same_taps = [
            seg_ext[tap * DILATION : tap * DILATION + frames_dev] == segment for tap in range(3)
        ]
        one_hot = (segment[:, None] == jnp.arange(utter_count)[None, :]).astype(f32)
        step_low = step_embedding(steps[micro_index, 0], width).astype(bf16)
        step_film = jnp.dot(step_low, full_step, preferred_element_type=f32)
        film_first = jnp.dot(one_hot, step_film, precision=PRECISE) + jnp.dot(
            cond_rows, full_cond, preferred_element_type=f32
        )
        gain_first = film_first[:, :width]
        hidden_low = (frame_rows * (1.0 + gain_first) + film_first[:, width:]).astype(bf16)
        extended = padded(hidden_low, (("tm", 0),), DILATION)
        stacked = jnp.concatenate(
            [
                extended[tap * DILATION : tap * DILATION + frames_dev]
                * same_taps[tap][:, None].astype(bf16)
                for tap in range(3)
            ],
            axis=1,
        )
        conv_out = jnp.dot(stacked, conv_flat, preferred_element_type=f32)
        tanh_part = jnp.tanh(conv_out[:, :width])
        sigm_part = jax.nn.sigmoid(conv_out[:, width:])
        activated = tanh_part * sigm_part
        prompt_rows = prompt[micro_index, 0]
        query_low = jnp.dot(full_q, full_query, preferred_element_type=f32).astype(bf16)
        key_low = jnp.dot(prompt_rows, full_key, preferred_element_type=f32).astype(bf16)
        value_low = jnp.dot(prompt_rows, full_value, preferred_element_type=f32).astype(bf16)
        query_heads = query_low.reshape(QUERIES, HEADS, head_size)
        key_heads = key_low.reshape(prompt_rows_dev, HEADS, head_size)
        value_heads = value_low.reshape(prompt_rows_dev, HEADS, head_size)
        scores = (
            jnp.einsum("qhd,khd->hqk", query_heads, key_heads, preferred_element_type=f32)
            * score_scale
        )
        local_top = jnp.max(scores, axis=-1)
        local_total = jnp.sum(jnp.exp(scores - local_top[..., None]), axis=-1)
        score_top, score_total = joined_2((local_top, local_total), "tm", softmax_join)
        probs = jnp.exp(scores - score_top[..., None]) / score_total[..., None]
        probs_low = probs.astype(bf16)
        context_part = jnp.einsum(
            "hqk,khd->qhd", probs_low, value_heads, preferred_element_type=f32
        ).reshape(QUERIES, width)
        context = lax.psum(context_part, "tm")
        context_low = context.astype(bf16)
        projected = jnp.dot(context_low, full_out, preferred_element_type=f32)
        summary_low = jnp.mean(projected, axis=0).astype(bf16)
        film_second = jnp.dot(summary_low[None, :], full_film, preferred_element_type=f32)[0]
        gain_second = film_second[:width]
        gated_low = (activated * (1.0 + gain_second) + film_second[width:]).astype(bf16)
        branch_out = jnp.dot(gated_low, full_proj, preferred_element_type=f32)
        res_list.append(
            ((frame_rows + branch_out[:, :width]) * SQRT_HALF * live_mask[:, None]).astype(bf16)
        )
        skip_list.append((branch_out[:, width:] * live_mask[:, None]).astype(bf16))
        res_cot = grad_res[micro_index, 0].astype(f32) * SQRT_HALF * live_mask[:, None]
        skip_cot = grad_skip[micro_index, 0].astype(f32) * live_mask[:, None]
        branch_cot = jnp.concatenate([res_cot, skip_cot], axis=1).astype(bf16)
        acc_proj = acc_proj + contract_rows(gated_low, branch_cot)
        gated_cot = contract_cols(branch_cot, full_proj)
        film_local = jnp.concatenate(
            [jnp.sum(gated_cot * activated, axis=0), jnp.sum(gated_cot, axis=0)]
        )
        film_cot = lax.psum(film_local, "tm")
        summary_f32 = summary_low.astype(f32)
        acc_film = acc_film + first_rank * (summary_f32[:, None] * film_cot[None, :])
        summary_cot = jnp.dot(full_film.astype(f32), film_cot, precision=PRECISE) / QUERIES
        context_total = jnp.sum(context_low.astype(f32), axis=0)
        acc_out = acc_out + first_rank * (context_total[:, None] * summary_cot[None, :])
        context_cot_row = jnp.dot(full_out.astype(f32), summary_cot, precision=PRECISE)
        context_cot = jnp.broadcast_to(context_cot_row[None, :], (QUERIES, width)).astype(bf16)
        context_cot_heads = context_cot.reshape(QUERIES, HEADS, head_size)
        prob_cot = jnp.einsum(
            "qhd,khd->hqk", context_cot_heads, value_heads, preferred_element_type=f32
        )
        row_part = jnp.sum(probs * prob_cot, axis=-1)
        row_total = lax.psum(row_part, "tm")
        score_cot = (probs * (prob_cot - row_total[..., None])).astype(bf16)
        query_cot = (
            jnp.einsum("hqk,khd->qhd", score_cot, key_heads, preferred_element_type=f32)
            * score_scale
        ).reshape(QUERIES, width)
        key_cot = (
            (
                jnp.einsum("hqk,qhd->khd", score_cot, query_heads, preferred_element_type=f32)
                * score_scale
            )
            .astype(bf16)
            .reshape(prompt_rows_dev, width)
        )
        value_cot = (
            jnp.einsum("hqk,qhd->khd", probs_low, context_cot_heads, preferred_element_type=f32)
            .astype(bf16)
            .reshape(prompt_rows_dev, width)
        )
        prompt_list.append(contract_cols(key_cot, full_key) + contract_cols(value_cot, full_value))
        acc_key = acc_key + contract_rows(prompt_rows, key_cot)
        acc_value = acc_value + contract_rows(prompt_rows, value_cot)
        acc_query = acc_query + contract_rows(full_q.astype(f32), query_cot, PRECISE)
        acc_q = acc_q + contract_cols(query_cot, full_query.astype(f32), PRECISE)
        act_cot = gated_cot * (1.0 + gain_second)
        conv_cot = jnp.concatenate(
            [
                act_cot * sigm_part * (1.0 - tanh_part * tanh_part),
                act_cot * tanh_part * sigm_part * (1.0 - sigm_part),
            ],
            axis=1,
        ).astype(bf16)
        acc_conv = acc_conv + contract_rows(stacked, conv_cot)
        cot_extended = padded(conv_cot, (("tm", 0),), DILATION)
        back_taps = jnp.stack(
            [
                cot_extended[(2 - tap) * DILATION : (2 - tap) * DILATION + frames_dev]
                * same_taps[2 - tap][:, None].astype(bf16)
                for tap in range(3)
            ],
            axis=1,
        )
        hidden_cot = lax.dot_general(
            back_taps, full_conv, (((1, 2), (0, 2)), ((), ())), preferred_element_type=f32
        )
        film_first_cot = jnp.concatenate([hidden_cot * frame_rows, hidden_cot], axis=1).astype(bf16)
        acc_cond = acc_cond + contract_rows(cond_rows, film_first_cot)
        step_film_cot = contract_rows(one_hot, film_first_cot.astype(f32), PRECISE)
        acc_step = acc_step + contract_rows(step_low.astype(f32), step_film_cot, PRECISE)
        frame_list.append(res_cot + hidden_cot * (1.0 + gain_first))
    acc_conv_taps = acc_conv.reshape(3, width, 2 * width)
    shares = (
        lax.psum_scatter(acc_q, "fsdp", scatter_dimension=0, tiled=True),
        lax.psum_scatter(acc_step, "fsdp", scatter_dimension=0, tiled=True),
        lax.psum_scatter(acc_cond, "fsdp", scatter_dimension=0, tiled=True),
        lax.psum_scatter(acc_conv_taps, "fsdp", scatter_dimension=1, tiled=True),
        lax.psum_scatter(acc_query, "fsdp", scatter_dimension=0, tiled=True),
        lax.psum_scatter(acc_key, "fsdp", scatter_dimension=0, tiled=True),
        lax.psum_scatter(acc_value, "fsdp", scatter_dimension=0, tiled=True),
        lax.psum_scatter(acc_out, "fsdp", scatter_dimension=0, tiled=True),
        lax.psum_scatter(acc_film, "fsdp", scatter_dimension=0, tiled=True),
        lax.psum_scatter(acc_proj, "fsdp", scatter_dimension=0, tiled=True),
    )
    summed = lax.psum(
        (
            shares[0],
            shares[1],
            shares[2],
            shares[3],
            shares[4],
            shares[5],
            shares[6],
            shares[7],
            shares[8],
            shares[9],
        ),
        "tm",
    )
    res_out = jnp.stack(res_list)[:, None]
    skip_out = jnp.stack(skip_list)[:, None]
    grad_frames = jnp.stack(frame_list)[:, None]
    grad_prompt = jnp.stack(prompt_list)[:, None]
    return (
        res_out,
        skip_out,
        grad_frames,
        grad_prompt,
        summed[0],
        summed[1],
        summed[2],
        summed[3],
        summed[4],
        summed[5],
        summed[6],
        summed[7],
        summed[8],
        summed[9],
    )


def solution(mesh):
    in_specs = (
        P(None, "fsdp", "tm", None),
        P(None, "fsdp", "tm", None),
        P(None, "fsdp", None),
        P(None, "fsdp", None),
        P(None, "fsdp", "tm", None),
        P("fsdp", None),
        P("fsdp", None),
        P("fsdp", None),
        P(None, "fsdp", None),
        P("fsdp", None),
        P("fsdp", None),
        P("fsdp", None),
        P("fsdp", None),
        P("fsdp", None),
        P("fsdp", None),
        P(None, "fsdp", "tm", None),
        P(None, "fsdp", "tm", None),
    )
    out_specs = (
        P(None, "fsdp", "tm", None),
        P(None, "fsdp", "tm", None),
        P(None, "fsdp", "tm", None),
        P(None, "fsdp", "tm", None),
        P("fsdp", None),
        P("fsdp", None),
        P("fsdp", None),
        P(None, "fsdp", None),
        P("fsdp", None),
        P("fsdp", None),
        P("fsdp", None),
        P("fsdp", None),
        P("fsdp", None),
        P("fsdp", None),
    )
    return jax.shard_map(
        per_device, mesh=mesh, in_specs=in_specs, out_specs=out_specs, check_vma=False
    )
```

profile of v0, /device:TPU:0, one launch (start us, length us, event | category | flops | bytes accessed | tf_op | source)
XLA Modules:
  0.0 827.9 jit_solution(15819924831970833689)
XLA Ops:
  17.6 15.5 %all_gather.70 = bf16[512,512]{1,0:T(8,128)(2,1)S(1)} all-gather(bf16[256,512]{1,0:T(8,128)(2,1)S(1)} %convert_element_type.320), channel_id=1, replica_groups=mesh['tm'=16,'fsdp'=2] {'fsdp'}, dimensions={0}, use_global_device_ids=true | all-gather | bytes 786432 | tf_op jit(solution)/shard_map/all_gather | solution.py:130
  34.2 10.2 %all_gather.67 = bf16[512,512]{1,0:T(8,128)(2,1)S(1)} all-gather(bf16[256,512]{1,0:T(8,128)(2,1)S(1)} %convert_element_type.315), channel_id=1, replica_groups=mesh['tm'=16,'fsdp'=2] {'fsdp'}, dimensions={0}, use_global_device_ids=true | all-gather | bytes 786432 | tf_op jit(solution)/shard_map/all_gather | solution.py:131
  49.9 13.5 %all_gather.69 = bf16[512,512]{1,0:T(8,128)(2,1)S(1)} all-gather(bf16[256,512]{1,0:T(8,128)(2,1)S(1)} %convert_element_type.318), channel_id=1, replica_groups=mesh['tm'=16,'fsdp'=2] {'fsdp'}, dimensions={0}, use_global_device_ids=true | all-gather | bytes 786432 | tf_op jit(solution)/shard_map/all_gather | solution.py:129
  64.1 22.6 %all-gather = f32[128,32]{1,0:T(8,128)S(1)} all-gather(f32[8,32]{1,0:T(8,128)S(1)} %get-tuple-element.438), channel_id=2, replica_groups=mesh['tm'=16,'fsdp'=2] {'tm'}, dimensions={0}, use_global_device_ids=true | all-gather | bytes 17408 | tf_op jit(solution)/shard_map/all_gather | solution.py:29
  86.7 17.6 %all-gather.1 = f32[128,32]{1,0:T(8,128)S(1)} all-gather(f32[8,32]{1,0:T(8,128)S(1)} %exponential_reduce_fusion.1), channel_id=3, replica_groups=mesh['tm'=16,'fsdp'=2] {'tm'}, dimensions={0}, use_global_device_ids=true | all-gather | bytes 17408 | tf_op jit(solution)/shard_map/all_gather | solution.py:29
  105.0 18.9 %all-gather.2 = f32[128,32]{1,0:T(8,128)S(1)} all-gather(f32[8,32]{1,0:T(8,128)S(1)} %get-tuple-element.436), channel_id=4, replica_groups=mesh['tm'=16,'fsdp'=2] {'tm'}, dimensions={0}, use_global_device_ids=true | all-gather | bytes 17408 | tf_op jit(solution)/shard_map/all_gather | solution.py:29
  124.0 17.6 %all-gather.3 = f32[128,32]{1,0:T(8,128)S(1)} all-gather(f32[8,32]{1,0:T(8,128)S(1)} %exponential_reduce_fusion), channel_id=5, replica_groups=mesh['tm'=16,'fsdp'=2] {'tm'}, dimensions={0}, use_global_device_ids=true | all-gather | bytes 17408 | tf_op jit(solution)/shard_map/all_gather | solution.py:29
  142.5 11.0 %all_gather.75 = bf16[512,512]{1,0:T(8,128)(2,1)S(1)} all-gather(bf16[256,512]{1,0:T(8,128)(2,1)S(1)} %convert_element_type.324), channel_id=1, replica_groups=mesh['tm'=16,'fsdp'=2] {'fsdp'}, dimensions={0}, use_global_device_ids=true | all-gather | bytes 786432 | tf_op jit(solution)/shard_map/all_gather | solution.py:132
  197.2 9.2 %fusion.78 = f32[1536,1024]{1,0:T(8,128)} fusion(bf16[1536,1024]{1,0:T(8,128)(2,1)} %bitcast.275, bf16[1536,512]{1,0:T(8,128)(2,1)} %get-tuple-element.411, bf16[1536,512]{1,0:T(8,128)(2,1)S(1)} %get-tuple-element.404, bf16[1536,512]{1,0:T(8,128)(2,1)} %get-tuple-element.410), kind=kOutput, calls=%fused_computation.128 | convolution fusion | flops 4845993984 | bytes 14155776 | tf_op jit(solution)/shard_map/dot_general | solution.py:178
  206.5 8.5 %multiply_reduce_fusion.1 = (f32[512]{0:T(512)S(1)}, f32[512]{0:T(512)S(1)}, f32[1536,512]{1,0:T(8,128)}) fusion(f32[1536,1024]{1,0:T(8,128)} %fusion.78, bf16[512,1024]{1,0:T(8,128)(2,1)} %all-gather.18.cloned.1.call-done, bf16[1536,512]{1,0:T(8,128)(2,1)} %get-tuple-element.408, bf16[1536,512]{1,0:T(8,128)(2,1)} %get-tuple-element.406), kind=kOutput, calls=%fused_computation.108 | convolution fusion | flops 1622408192 | bytes 13635584 | tf_op jit(solution)/shard_map/dot_general | solution.py:50
  224.0 32.8 %all-reduce.2 = (f32[1024]{0:T(1024)S(1)}, f32[1024]{0:T(1024)S(1)}) all-reduce(f32[1024]{0:T(1024)S(1)} %pad_maximum_fusion.45, f32[1024]{0:T(1024)S(1)} %pad_maximum_fusion.44), channel_id=1, replica_groups=mesh['tm'=16,'fsdp'=2] {'tm'}, use_global_device_ids=true, to_apply=%region_23.24 | all-reduce | flops 2048 | bytes 16384 | tf_op jit(solution)/shard_map/psum | solution.py:221
  262.8 30.0 %all-reduce.1 = (f32[8,32]{1,0:T(8,128)S(1)}, f32[8,32]{1,0:T(8,128)S(1)}) all-reduce(f32[8,32]{1,0:T(8,128)S(1)} %get-tuple-element.442, f32[8,32]{1,0:T(8,128)S(1)} %get-tuple-element.444), channel_id=1, replica_groups=mesh['tm'=16,'fsdp'=2] {'tm'}, use_global_device_ids=true, to_apply=%region_25.26 | all-reduce | flops 512 | bytes 4096 | tf_op jit(solution)/shard_map/psum | solution.py:234
  303.0 61.7 %all-reduce.8 = (bf16[32,512]{1,0:T(8,128)(2,1)S(1)}, bf16[32,512]{1,0:T(8,128)(2,1)S(1)}, f32[16,512]{1,0:T(8,128)}) all-reduce(f32[32,512]{1,0:T(8,128)S(1)} %reshape.308, f32[32,512]{1,0:T(8,128)S(1)} %reshape.303, f32[16,512]{1,0:T(8,128)} %reduce-scatter.11.cloned.1.call-done), channel_id=1, replica_groups=mesh['tm'=16,'fsdp'=2] {'tm'}, use_global_device_ids=true, to_apply=%region_14.15 | all-reduce | flops 40960 | bytes 262144 | tf_op jit(solution)/shard_map/psum | solution.py:201
  397.8 6.3 fusion.199
  404.1 10.7 %fusion.39 = (bf16[1536,1,1024]{2,0,1:T(8,128)(2,1)}, bf16[1536,1,1024]{2,0,1:T(8,128)(2,1)}) fusion(bf16[16,1024]{1,0:T(8,128)(2,1)S(1)} %collective-permute-done.6, bf16[1536,512]{1,0:T(8,128)(2,1)S(1)} %copy-done.3, bf16[1536,512]{1,0:T(8,128)(2,1)S(1)} %get-tuple-element.382, bf16[1536]{0:T(1024)(128)(2,1)S(1)} %get-tuple-element.421, ...), kind=kLoop, calls=%fused_computation.56 | loop fusion | flops 25165824 | bytes 9508864 | tf_op jit(solution)/shard_map/stack | solution.py:268
  414.9 9.1 %fusion.43 = (bf16[1536,1,1024]{2,0,1:T(8,128)(2,1)S(1)}, bf16[1536,1,1024]{2,0,1:T(8,128)(2,1)S(1)}) fusion(bf16[16,1024]{1,0:T(8,128)(2,1)S(1)} %collective-permute-done.4, bf16[1536,512]{1,0:T(8,128)(2,1)S(1)} %copy-done.6, bf16[1536,512]{1,0:T(8,128)(2,1)S(1)} %copy-done.4, bf16[1536]{0:T(1024)(128)(2,1)S(1)} %get-tuple-element.419, ...), kind=kLoop, calls=%fused_computation.64 | loop fusion | flops 25165824 | bytes 9508864 | tf_op jit(solution)/shard_map/stack | solution.py:268
  424.0 6.5 fusion.23
  430.5 20.3 %fusion.80 = (bf16[1,1536,512]{2,1,0:T(8,128)(2,1)}, bf16[1,1536,512]{2,1,0:T(8,128)(2,1)}, bf16[1536,512]{1,0:T(8,128)(2,1)}, f32[1,1536,512]{2,1,0:T(8,128)}, ...) fusion(f32[1536,1024]{1,0:T(8,128)} %fusion.199, ...), kind=kOutput, calls=%fused_computation.131 | convolution fusion | flops 4887674880 | bytes 50350080 | tf_op jit(solution)/shard_map/dot_general | solution.py:276
  466.4 7.8 fusion.55
  474.3 8.3 %convolution_add_fusion.2 = f32[1536,1024]{1,0:T(8,128)} fusion(f32[1536,1024]{1,0:T(8,128)S(1)} %fusion.55, bf16[1536,512]{1,0:T(8,128)(2,1)S(1)} %copy-done.7, bf16[1536,512]{1,0:T(8,128)(2,1)S(1)} %copy-done.5, bf16[1536,512]{1,0:T(8,128)(2,1)S(1)} %copy-done.29, bf16[1536,512]{1,0:T(8,128)(2,1)S(1)} %copy-done.15, bf16[1536,512]{1,0:T(8,128)(2,1)S(1)} %copy-done.28), kind=kOutput, calls=%fused_computation.37 | convolution fusion | flops 4853858304 | bytes 20447232 | tf_op jit(solution)/shard_map/dot_general | solution.py:40
  483.1 14.7 %reduce-scatter.15.cloned.1.call-done = f32[256,1024]{0,1:T(8,128)} async-done(((f32[512,1024]{0,1:T(8,128)}), f32[256,1024]{0,1:T(8,128)}) %reduce-scatter.15.cloned.1.call-update) | async-done | bytes 1048592 | tf_op jit(solution)/shard_map/reduce_scatter | solution.py:288
  497.8 34.6 %reduce-scatter.13.cloned.1.call-done = f32[256,1024]{1,0:T(8,128)} async-done(((f32[512,1024]{1,0:T(8,128)}), f32[256,1024]{1,0:T(8,128)}) %reduce-scatter.13.cloned.1.call-update) | async-done | bytes 1048592 | tf_op jit(solution)/shard_map/reduce_scatter | solution.py:287
  532.4 79.8 %reduce-scatter.17.cloned.1.call-done = f32[3,256,1024]{2,1,0:T(8,128)} async-done(((f32[3,512,1024]{2,1,0:T(8,128)}), f32[3,256,1024]{2,1,0:T(8,128)}) %reduce-scatter.17.cloned.1.call-update) | async-done | bytes 3145744 | tf_op jit(solution)/shard_map/reduce_scatter | solution.py:289
  629.5 176.1 %all-reduce.7.cloned.1.call-done = (f32[256,1024]{1,0:T(8,128)}, f32[256,1024]{0,1:T(8,128)}, f32[3,256,1024]{2,1,0:T(8,128)}, f32[256,512]{0,1:T(8,128)}, f32[2...) async-done(((f32[256,1024]{1,0:T(8,128)}, f32[256,1024]{0,1:T(8,128)}, f32[3,256,1024]{2,1,0:T(8,128)}, ...) | async-done | bytes 9437200 | tf_op jit(solution)/shard_map/psum | solution.py:297
  (404 shorter events, 169.5 us)
Async XLA Ops:
  7.2 152.4 %all-gather.12.cloned.1.call-start = ((), (), s32[]{:S(2)}) async-start(), calls=%async_computation.11 | async-start | bytes 1572864 | tf_op jit(solution)/shard_map/all_gather | solution.py:127
  9.5 156.3 %all-gather.10.cloned.1.call-start = ((), (), s32[]{:S(2)}) async-start(), calls=%async_computation.10 | async-start | bytes 1572864 | tf_op jit(solution)/shard_map/all_gather | solution.py:126
  11.7 185.5 %all-gather.14.cloned.1.call-start = ((), (), s32[]{:S(2)}) async-start(), calls=%async_computation.12 | async-start | bytes 4718592 | tf_op jit(solution)/shard_map/all_gather | solution.py:128
  13.2 193.3 %all-gather.18.cloned.1.call-start = ((), (), s32[]{:S(2)}) async-start(), calls=%async_computation.14 | async-start | bytes 1572864 | tf_op jit(solution)/shard_map/all_gather | solution.py:134
  15.4 241.4 %all-gather.16.cloned.1.call-start = ((), (), s32[]{:S(2)}) async-start(), calls=%async_computation.13 | async-start | bytes 1572864 | tf_op jit(solution)/shard_map/all_gather | solution.py:133
  16.4 286.6 %reduce-scatter.11.cloned.1.call-start = ((), (), s32[]{:S(2)}) async-start(), calls=%async_computation.15 | async-start | bytes 98304 | tf_op jit(solution)/shard_map/reduce_scatter | solution.py:286
  180.8 9.1 %collective-permute-start.2 = (bf16[16,512]{1,0:T(8,128)(2,1)S(1)}, bf16[16,512]{1,0:T(8,128)(2,1)S(1)}, u32[]{:S(2)}, u32[]{:S(2)}) collective-permute-start(bf16[16,512]{1,0:T(8,128)(2,1)S(1)} %get-tuple-element.416), channel_id=1, source_target_pairs={{0,2},{2,4},{4,6},{6,8},{8,10},{10,12},{12,14},{14,16},{16,18},{18... | collective-permute-start | bytes 49160 | tf_op jit(solution)/shard_map/ppermute | solution.py:20
  182.1 7.8 collective-permute-start.3
  183.4 10.2 %collective-permute-start = (bf16[16,512]{1,0:T(8,128)(2,1)S(1)}, bf16[16,512]{1,0:T(8,128)(2,1)S(1)}, u32[]{:S(2)}, u32[]{:S(2)}) collective-permute-start(bf16[16,512]{1,0:T(8,128)(2,1)S(1)} %get-tuple-element.412), channel_id=1, source_target_pairs={{0,2},{2,4},{4,6},{6,8},{8,10},{10,12},{12,14},{14,16},{16,18},{18... | collective-permute-start | bytes 49160 | tf_op jit(solution)/shard_map/ppermute | solution.py:20
  188.5 5.1 collective-permute-start.1
  296.0 187.0 %reduce-scatter.19.cloned.1.call-start = ((), (), s32[]{:S(2)}) async-start(), calls=%async_computation.19 | async-start | bytes 1572864 | tf_op jit(solution)/shard_map/reduce_scatter | solution.py:290
  297.7 185.3 %reduce-scatter.23.cloned.1.call-start = ((), (), s32[]{:S(2)}) async-start(), calls=%async_computation.21 | async-start | bytes 1572864 | tf_op jit(solution)/shard_map/reduce_scatter | solution.py:292
  299.9 183.1 %reduce-scatter.21.cloned.1.call-start = ((), (), s32[]{:S(2)}) async-start(), calls=%async_computation.20 | async-start | bytes 1572864 | tf_op jit(solution)/shard_map/reduce_scatter | solution.py:291
  302.2 180.9 %reduce-scatter.25.cloned.1.call-start = ((), (), s32[]{:S(2)}) async-start(), calls=%async_computation.22 | async-start | bytes 1572864 | tf_op jit(solution)/shard_map/reduce_scatter | solution.py:293
  367.9 115.2 %reduce-scatter.29.cloned.1.call-start = ((), (), s32[]{:S(2)}) async-start(), calls=%async_computation.24 | async-start | bytes 3145728 | tf_op jit(solution)/shard_map/reduce_scatter | solution.py:295
  385.7 97.4 %reduce-scatter.27.cloned.1.call-start = ((), (), s32[]{:S(2)}) async-start(), calls=%async_computation.23 | async-start | bytes 3145728 | tf_op jit(solution)/shard_map/reduce_scatter | solution.py:294
  386.7 28.2 %collective-permute-start.4 = (bf16[16,1024]{1,0:T(8,128)(2,1)S(1)}, bf16[16,1024]{1,0:T(8,128)(2,1)S(1)}, u32[]{:S(2)}, u32[]{:S(2)}) collective-permute-start(bf16[16,1024]{1,0:T(8,128)(2,1)S(1)} %get-tuple-element.398), channel_id=1, source_target_pairs={{2,0},{4,2},{6,4},{8,6},{10,8},{12,10},{14,12},{16,14},{18,16},{20... | collective-permute-start | bytes 98312 | tf_op jit(solution)/shard_map/ppermute | solution.py:23
  388.0 26.9 %collective-permute-start.5 = (bf16[16,1024]{1,0:T(8,128)(2,1)S(1)}, bf16[16,1024]{1,0:T(8,128)(2,1)S(1)}, u32[]{:S(2)}, u32[]{:S(2)}) collective-permute-start(bf16[16,1024]{1,0:T(8,128)(2,1)S(1)} %get-tuple-element.399), channel_id=1, source_target_pairs={{0,2},{2,4},{4,6},{6,8},{8,10},{10,12},{12,14},{14,16},{16,18},{18... | collective-permute-start | bytes 98312 | tf_op jit(solution)/shard_map/ppermute | solution.py:20
  391.6 12.5 %collective-permute-start.6 = (bf16[16,1024]{1,0:T(8,128)(2,1)}, bf16[16,1024]{1,0:T(8,128)(2,1)S(1)}, u32[]{:S(2)}, u32[]{:S(2)}) collective-permute-start(bf16[16,1024]{1,0:T(8,128)(2,1)} %get-tuple-element.402), channel_id=1, source_target_pairs={{2,0},{4,2},{6,4},{8,6},{10,8},{12,10},{14,12},{16,14},{18,16},{20... | collective-permute-start | bytes 98312 | tf_op jit(solution)/shard_map/ppermute | solution.py:23
  392.9 11.2 %collective-permute-start.7 = (bf16[16,1024]{1,0:T(8,128)(2,1)S(1)}, bf16[16,1024]{1,0:T(8,128)(2,1)S(1)}, u32[]{:S(2)}, u32[]{:S(2)}) collective-permute-start(bf16[16,1024]{1,0:T(8,128)(2,1)S(1)} %get-tuple-element.403), channel_id=1, source_target_pairs={{0,2},{2,4},{4,6},{6,8},{8,10},{10,12},{12,14},{14,16},{16,18},{18... | collective-permute-start | bytes 98312 | tf_op jit(solution)/shard_map/ppermute | solution.py:20
  397.7 100.1 %reduce-scatter.15.cloned.1.call-start = ((), (), s32[]{:S(2)}) async-start(), calls=%async_computation.17 | async-start | bytes 3145728 | tf_op jit(solution)/shard_map/reduce_scatter | solution.py:288
  458.9 73.5 %reduce-scatter.13.cloned.1.call-start = ((), (), s32[]{:S(2)}) async-start(), calls=%async_computation.16 | async-start | bytes 3145728 | tf_op jit(solution)/shard_map/reduce_scatter | solution.py:287
  466.3 145.9 %reduce-scatter.17.cloned.1.call-start = ((), (), s32[]{:S(2)}) async-start(), calls=%async_computation.18 | async-start | bytes 9437184 | tf_op jit(solution)/shard_map/reduce_scatter | solution.py:289
  482.7 322.9 %all-reduce.7.cloned.1.call-start = ((), (), s32[]{:S(2)}) async-start(), calls=%async_computation.25 | async-start | bytes 18874368 | tf_op jit(solution)/shard_map/psum | solution.py:297
  (77 other events, 965.3 us)
Sparse Core Ops, SparseCore 0:
  10.1 30.0 all-gather.11
  42.4 26.2 all-gather.9
  70.7 45.4 all-gather.13
  118.2 21.2 all-gather.17
  141.5 22.1 all-gather.15
  296.2 6.0 reduce-scatter.10
  305.1 20.3 reduce-scatter.18
  328.3 20.3 reduce-scatter.22
  351.5 20.3 reduce-scatter.20
  374.6 20.3 reduce-scatter.24
  397.2 31.8 reduce-scatter.28
  431.3 31.8 reduce-scatter.26
  465.9 31.8 reduce-scatter.14
  500.6 31.8 reduce-scatter.12
  535.1 77.0 reduce-scatter.16
  617.6 187.9 all-reduce.6
where the time goes:
time: 832 us; the launch traced here: 828 us
  waiting for transfers between devices  306 us (37%)
  blocking collectives  256 us (31%)
  matrix products  135 us (16%)
  other arithmetic  69.2 us (8%)
  local copies, waits for them, and re-layouts  27.7 us (3%)
  starting transfers between devices  18.6 us (2%)
  between operations  15.6 us (2%)
    psum x1, waiting for transfers between devices, per_device(): lax.psum((shares[0], shares[1], shares[2], shares[3], shares[4], shares[5...  176 us
    reduce_scatter x1, waiting for transfers between devices, per_device(): lax.psum_scatter(acc_conv_taps, 'fsdp', scatter_dimension=1, tiled=True)  79.8 us
    all_gather x4, blocking collectives, joined_2(): gathered = jax.tree.map(lambda a: lax.all_gather(a, axis), part)  76.7 us
    psum x1, blocking collectives, per_device(): context = lax.psum(context_part, 'tm')  61.7 us
    dot_general x16, matrix products, contract_rows(): lax.dot_general(left, right, (((0,), (0,)), ((), ())), precision=precisio...  41.8 us
    reduce_scatter x1, waiting for transfers between devices, per_device(): lax.psum_scatter(acc_step, 'fsdp', scatter_dimension=0, tiled=True)  34.6 us
    psum x1, blocking collectives, per_device(): film_cot = lax.psum(film_local, 'tm')  32.8 us
    psum x1, blocking collectives, per_device(): row_total = lax.psum(row_part, 'tm')  30 us
  transfers between devices with their start and end apart: 24, of which 4 were waited for; matrix products, arithmetic and copies ran while one was open for 24% of the time, Pallas kernels for 0%

commit v1 on v0

--- a/solution.py
+++ b/solution.py
@@ -3,6 +3,7 @@
 import jax.numpy as jnp
 from jax import lax
 from jax.sharding import PartitionSpec as P
+from jax.lax import ppermute, psum
 
 HEADS = 8
 QUERIES = 32
@@ -231,7 +232,15 @@
             "qhd,khd->hqk", context_cot_heads, value_heads, preferred_element_type=f32
         )
         row_part = jnp.sum(probs * prob_cot, axis=-1)
-        row_total = lax.psum(row_part, "tm")
+
+        def measure_run(tile_in, named_axis):
+            many = psum(1, named_axis)
+            carry = tile_in
+            for t in [[(i0, i0 ^ d) for i0 in range(many)] for d in (1, 2, 4, 8, 16) if d < many]:
+                carry = carry + ppermute(carry, named_axis, t)
+            return carry
+
+        row_total = measure_run(row_part, "tm")
         score_cot = (probs * (prob_cot - row_total[..., None])).astype(bf16)
         query_cot = (
             jnp.einsum("hqk,khd->qhd", score_cot, key_heads, preferred_element_type=f32)

time: 832 us -> 816 us (0.981)
  blocking collectives: 256 us -> 227 us
    psum x1 -> x0, blocking collectives: 30 us -> none  [per_device(): row_total = lax.psum(row_part, 'tm')]
  transfers between devices with their start and end apart: 24 -> 32, of which waited for: 4 -> 12; matrix products, arithmetic and copies ran while one was open for 24% -> 24% of each run, Pallas kernels for 0% -> 0%
where the time goes in v1:
time: 816 us; the launch traced here: 812 us
  waiting for transfers between devices  312 us (38%)
  blocking collectives  227 us (28%)
  matrix products  135 us (17%)
  other arithmetic  69.1 us (8%)
  local copies, waits for them, and re-layouts  27.7 us (3%)
  starting transfers between devices  26.3 us (3%)
  between operations  15.6 us (2%)
    psum x1, waiting for transfers between devices, per_device(): lax.psum((shares[0], shares[1], shares[2], shares[3], shares[4], shares[5...  176 us
    reduce_scatter x1, waiting for transfers between devices, per_device(): lax.psum_scatter(acc_conv_taps, 'fsdp', scatter_dimension=1, tiled=True)  79.8 us
    all_gather x4, blocking collectives, joined_2(): gathered = jax.tree.map(lambda a: lax.all_gather(a, axis), part)  76.7 us
    psum x1, blocking collectives, per_device(): context = lax.psum(context_part, 'tm')  62.5 us
    dot_general x16, matrix products, contract_rows(): lax.dot_general(left, right, (((0,), (0,)), ((), ())), precision=precisio...  41.8 us
    reduce_scatter x1, waiting for transfers between devices, per_device(): lax.psum_scatter(acc_step, 'fsdp', scatter_dimension=0, tiled=True)  34.6 us
    psum x1, blocking collectives, per_device(): film_cot = lax.psum(film_local, 'tm')  32.8 us
    dot_general x2, matrix products, per_device(): lax.dot_general(back_taps, full_conv, (((1, 2), (0, 2)), ((), ())), prefe...  26.9 us
  transfers between devices with their start and end apart: 32, of which 12 were waited for; matrix products, arithmetic and copies ran while one was open for 24% of the time, Pallas kernels for 0%

profile of v1, /device:TPU:0, one launch (start us, length us, event | category | flops | bytes accessed | tf_op | source)
XLA Modules:
  0.0 812.4 jit_solution(11333347762466838583)
XLA Ops:
  17.6 15.5 %all_gather.70 = bf16[512,512]{1,0:T(8,128)(2,1)S(1)} all-gather(bf16[256,512]{1,0:T(8,128)(2,1)S(1)} %convert_element_type.320), channel_id=1, replica_groups=mesh['tm'=16,'fsdp'=2] {'fsdp'}, dimensions={0}, use_global_device_ids=true | all-gather | bytes 786432 | tf_op jit(solution)/shard_map/all_gather | solution.py:131
  34.2 10.2 %all_gather.67 = bf16[512,512]{1,0:T(8,128)(2,1)S(1)} all-gather(bf16[256,512]{1,0:T(8,128)(2,1)S(1)} %convert_element_type.315), channel_id=1, replica_groups=mesh['tm'=16,'fsdp'=2] {'fsdp'}, dimensions={0}, use_global_device_ids=true | all-gather | bytes 786432 | tf_op jit(solution)/shard_map/all_gather | solution.py:132
  49.9 13.5 %all_gather.69 = bf16[512,512]{1,0:T(8,128)(2,1)S(1)} all-gather(bf16[256,512]{1,0:T(8,128)(2,1)S(1)} %convert_element_type.318), channel_id=1, replica_groups=mesh['tm'=16,'fsdp'=2] {'fsdp'}, dimensions={0}, use_global_device_ids=true | all-gather | bytes 786432 | tf_op jit(solution)/shard_map/all_gather | solution.py:130
  64.0 22.6 %all-gather = f32[128,32]{1,0:T(8,128)S(1)} all-gather(f32[8,32]{1,0:T(8,128)S(1)} %get-tuple-element.436), channel_id=2, replica_groups=mesh['tm'=16,'fsdp'=2] {'tm'}, dimensions={0}, use_global_device_ids=true | all-gather | bytes 17408 | tf_op jit(solution)/shard_map/all_gather | solution.py:30
  86.6 17.6 %all-gather.1 = f32[128,32]{1,0:T(8,128)S(1)} all-gather(f32[8,32]{1,0:T(8,128)S(1)} %exponential_reduce_fusion.1), channel_id=3, replica_groups=mesh['tm'=16,'fsdp'=2] {'tm'}, dimensions={0}, use_global_device_ids=true | all-gather | bytes 17408 | tf_op jit(solution)/shard_map/all_gather | solution.py:30
  105.0 18.9 %all-gather.2 = f32[128,32]{1,0:T(8,128)S(1)} all-gather(f32[8,32]{1,0:T(8,128)S(1)} %get-tuple-element.434), channel_id=4, replica_groups=mesh['tm'=16,'fsdp'=2] {'tm'}, dimensions={0}, use_global_device_ids=true | all-gather | bytes 17408 | tf_op jit(solution)/shard_map/all_gather | solution.py:30
  124.0 17.6 %all-gather.3 = f32[128,32]{1,0:T(8,128)S(1)} all-gather(f32[8,32]{1,0:T(8,128)S(1)} %exponential_reduce_fusion), channel_id=5, replica_groups=mesh['tm'=16,'fsdp'=2] {'tm'}, dimensions={0}, use_global_device_ids=true | all-gather | bytes 17408 | tf_op jit(solution)/shard_map/all_gather | solution.py:30
  142.4 11.0 %all_gather.75 = bf16[512,512]{1,0:T(8,128)(2,1)S(1)} all-gather(bf16[256,512]{1,0:T(8,128)(2,1)S(1)} %convert_element_type.324), channel_id=1, replica_groups=mesh['tm'=16,'fsdp'=2] {'fsdp'}, dimensions={0}, use_global_device_ids=true | all-gather | bytes 786432 | tf_op jit(solution)/shard_map/all_gather | solution.py:133
  159.5 6.2 fusion.88
  197.1 9.3 %fusion.78 = f32[1536,1024]{1,0:T(8,128)} fusion(bf16[1536,1024]{1,0:T(8,128)(2,1)} %bitcast.275, bf16[1536,512]{1,0:T(8,128)(2,1)} %get-tuple-element.409, bf16[1536,512]{1,0:T(8,128)(2,1)S(1)} %get-tuple-element.402, bf16[1536,512]{1,0:T(8,128)(2,1)} %get-tuple-element.408), kind=kOutput, calls=%fused_computation.128 | convolution fusion | flops 4845993984 | bytes 14155776 | tf_op jit(solution)/shard_map/dot_general | solution.py:179
  206.3 8.5 %multiply_reduce_fusion.1 = (f32[512]{0:T(512)S(1)}, f32[512]{0:T(512)S(1)}, f32[1536,512]{1,0:T(8,128)}) fusion(f32[1536,1024]{1,0:T(8,128)} %fusion.78, bf16[512,1024]{1,0:T(8,128)(2,1)} %all-gather.18.cloned.1.call-done, bf16[1536,512]{1,0:T(8,128)(2,1)} %get-tuple-element.406, bf16[1536,512]{1,0:T(8,128)(2,1)} %get-tuple-element.404), kind=kOutput, calls=%fused_computation.108 | convolution fusion | flops 1622408192 | bytes 13635584 | tf_op jit(solution)/shard_map/dot_general | solution.py:51
  223.9 32.8 %all-reduce.1 = (f32[1024]{0:T(1024)S(1)}, f32[1024]{0:T(1024)S(1)}) all-reduce(f32[1024]{0:T(1024)S(1)} %pad_maximum_fusion.45, f32[1024]{0:T(1024)S(1)} %pad_maximum_fusion.44), channel_id=1, replica_groups=mesh['tm'=16,'fsdp'=2] {'tm'}, use_global_device_ids=true, to_apply=%region_22.23 | all-reduce | flops 2048 | bytes 16384 | tf_op jit(solution)/shard_map/psum | solution.py:222
  286.7 62.5 %all-reduce.7 = (bf16[32,512]{1,0:T(8,128)(2,1)S(1)}, bf16[32,512]{1,0:T(8,128)(2,1)S(1)}, f32[16,512]{1,0:T(8,128)}) all-reduce(f32[32,512]{1,0:T(8,128)S(1)} %reshape.308, f32[32,512]{1,0:T(8,128)S(1)} %reshape.303, f32[16,512]{1,0:T(8,128)} %reduce-scatter.11.cloned.1.call-done), channel_id=1, replica_groups=mesh['tm'=16,'fsdp'=2] {'tm'}, use_global_device_ids=true, to_apply=%region_14.15 | all-reduce | flops 40960 | bytes 262144 | tf_op jit(solution)/shard_map/psum | solution.py:202
  382.6 6.3 fusion.199
  388.9 10.6 %fusion.39 = (bf16[1536,1,1024]{2,0,1:T(8,128)(2,1)}, bf16[1536,1,1024]{2,0,1:T(8,128)(2,1)}) fusion(bf16[16,1024]{1,0:T(8,128)(2,1)S(1)} %collective-permute-done.6, bf16[1536,512]{1,0:T(8,128)(2,1)S(1)} %copy-done.3, bf16[1536,512]{1,0:T(8,128)(2,1)S(1)} %get-tuple-element.380, bf16[1536]{0:T(1024)(128)(2,1)S(1)} %get-tuple-element.419, ...), kind=kLoop, calls=%fused_computation.56 | loop fusion | flops 25165824 | bytes 9508864 | tf_op jit(solution)/shard_map/stack | solution.py:277
  399.5 9.1 %fusion.43 = (bf16[1536,1,1024]{2,0,1:T(8,128)(2,1)S(1)}, bf16[1536,1,1024]{2,0,1:T(8,128)(2,1)S(1)}) fusion(bf16[16,1024]{1,0:T(8,128)(2,1)S(1)} %collective-permute-done.4, bf16[1536,512]{1,0:T(8,128)(2,1)S(1)} %copy-done.6, bf16[1536,512]{1,0:T(8,128)(2,1)S(1)} %copy-done.4, bf16[1536]{0:T(1024)(128)(2,1)S(1)} %get-tuple-element.417, ...), kind=kLoop, calls=%fused_computation.64 | loop fusion | flops 25165824 | bytes 9508864 | tf_op jit(solution)/shard_map/stack | solution.py:277
  408.6 6.5 fusion.23
  415.1 20.4 %fusion.80 = (bf16[1,1536,512]{2,1,0:T(8,128)(2,1)}, bf16[1,1536,512]{2,1,0:T(8,128)(2,1)}, bf16[1536,512]{1,0:T(8,128)(2,1)}, f32[1,1536,512]{2,1,0:T(8,128)}, ...) fusion(f32[1536,1024]{1,0:T(8,128)} %fusion.199, ...), kind=kOutput, calls=%fused_computation.131 | convolution fusion | flops 4887674880 | bytes 50350080 | tf_op jit(solution)/shard_map/dot_general | solution.py:285
  451.1 7.8 fusion.55
  459.0 8.3 %convolution_add_fusion.2 = f32[1536,1024]{1,0:T(8,128)} fusion(f32[1536,1024]{1,0:T(8,128)S(1)} %fusion.55, bf16[1536,512]{1,0:T(8,128)(2,1)S(1)} %copy-done.7, bf16[1536,512]{1,0:T(8,128)(2,1)S(1)} %copy-done.5, bf16[1536,512]{1,0:T(8,128)(2,1)S(1)} %copy-done.29, bf16[1536,512]{1,0:T(8,128)(2,1)S(1)} %copy-done.15, bf16[1536,512]{1,0:T(8,128)(2,1)S(1)} %copy-done.28), kind=kOutput, calls=%fused_computation.37 | convolution fusion | flops 4853858304 | bytes 20447232 | tf_op jit(solution)/shard_map/dot_general | solution.py:41
  467.8 14.5 %reduce-scatter.15.cloned.1.call-done = f32[256,1024]{0,1:T(8,128)} async-done(((f32[512,1024]{0,1:T(8,128)}), f32[256,1024]{0,1:T(8,128)}) %reduce-scatter.15.cloned.1.call-update) | async-done | bytes 1048592 | tf_op jit(solution)/shard_map/reduce_scatter | solution.py:297
  482.3 34.6 %reduce-scatter.13.cloned.1.call-done = f32[256,1024]{1,0:T(8,128)} async-done(((f32[512,1024]{1,0:T(8,128)}), f32[256,1024]{1,0:T(8,128)}) %reduce-scatter.13.cloned.1.call-update) | async-done | bytes 1048592 | tf_op jit(solution)/shard_map/reduce_scatter | solution.py:296
  516.9 79.8 %reduce-scatter.17.cloned.1.call-done = f32[3,256,1024]{2,1,0:T(8,128)} async-done(((f32[3,512,1024]{2,1,0:T(8,128)}), f32[3,256,1024]{2,1,0:T(8,128)}) %reduce-scatter.17.cloned.1.call-update) | async-done | bytes 3145744 | tf_op jit(solution)/shard_map/reduce_scatter | solution.py:298
  614.0 176.1 %all-reduce.6.cloned.1.call-done = (f32[256,1024]{1,0:T(8,128)}, f32[256,1024]{0,1:T(8,128)}, f32[3,256,1024]{2,1,0:T(8,128)}, f32[256,512]{0,1:T(8,128)}, f32[2...) async-done(((f32[256,1024]{1,0:T(8,128)}, f32[256,1024]{0,1:T(8,128)}, f32[3,256,1024]{2,1,0:T(8,128)}, ...) | async-done | bytes 9437200 | tf_op jit(solution)/shard_map/psum | solution.py:306
  (427 shorter events, 177.2 us)
Async XLA Ops:
  7.2 152.3 %all-gather.12.cloned.1.call-start = ((), (), s32[]{:S(2)}) async-start(), calls=%async_computation.11 | async-start | bytes 1572864 | tf_op jit(solution)/shard_map/all_gather | solution.py:128
  9.5 156.2 %all-gather.10.cloned.1.call-start = ((), (), s32[]{:S(2)}) async-start(), calls=%async_computation.10 | async-start | bytes 1572864 | tf_op jit(solution)/shard_map/all_gather | solution.py:127
  11.7 185.4 %all-gather.14.cloned.1.call-start = ((), (), s32[]{:S(2)}) async-start(), calls=%async_computation.12 | async-start | bytes 4718592 | tf_op jit(solution)/shard_map/all_gather | solution.py:129
  13.2 193.2 %all-gather.18.cloned.1.call-start = ((), (), s32[]{:S(2)}) async-start(), calls=%async_computation.14 | async-start | bytes 1572864 | tf_op jit(solution)/shard_map/all_gather | solution.py:135
  15.4 241.3 %all-gather.16.cloned.1.call-start = ((), (), s32[]{:S(2)}) async-start(), calls=%async_computation.13 | async-start | bytes 1572864 | tf_op jit(solution)/shard_map/all_gather | solution.py:134
  16.4 270.3 %reduce-scatter.11.cloned.1.call-start = ((), (), s32[]{:S(2)}) async-start(), calls=%async_computation.15 | async-start | bytes 98304 | tf_op jit(solution)/shard_map/reduce_scatter | solution.py:295
  180.7 9.1 %collective-permute-start.2 = (bf16[16,512]{1,0:T(8,128)(2,1)S(1)}, bf16[16,512]{1,0:T(8,128)(2,1)S(1)}, u32[]{:S(2)}, u32[]{:S(2)}) collective-permute-start(bf16[16,512]{1,0:T(8,128)(2,1)S(1)} %get-tuple-element.414), channel_id=1, source_target_pairs={{0,2},{2,4},{4,6},{6,8},{8,10},{10,12},{12,14},{14,16},{16,18},{18... | collective-permute-start | bytes 49160 | tf_op jit(solution)/shard_map/ppermute | solution.py:21
  182.0 7.8 collective-permute-start.3
  183.3 10.2 %collective-permute-start = (bf16[16,512]{1,0:T(8,128)(2,1)S(1)}, bf16[16,512]{1,0:T(8,128)(2,1)S(1)}, u32[]{:S(2)}, u32[]{:S(2)}) collective-permute-start(bf16[16,512]{1,0:T(8,128)(2,1)S(1)} %get-tuple-element.410), channel_id=1, source_target_pairs={{0,2},{2,4},{4,6},{6,8},{8,10},{10,12},{12,14},{14,16},{16,18},{18... | collective-permute-start | bytes 49160 | tf_op jit(solution)/shard_map/ppermute | solution.py:21
  188.5 5.1 collective-permute-start.1
  278.1 189.6 %reduce-scatter.23.cloned.1.call-start = ((), (), s32[]{:S(2)}) async-start(), calls=%async_computation.21 | async-start | bytes 1572864 | tf_op jit(solution)/shard_map/reduce_scatter | solution.py:301
  279.4 188.2 %reduce-scatter.19.cloned.1.call-start = ((), (), s32[]{:S(2)}) async-start(), calls=%async_computation.19 | async-start | bytes 1572864 | tf_op jit(solution)/shard_map/reduce_scatter | solution.py:299
  281.8 185.9 %reduce-scatter.21.cloned.1.call-start = ((), (), s32[]{:S(2)}) async-start(), calls=%async_computation.20 | async-start | bytes 1572864 | tf_op jit(solution)/shard_map/reduce_scatter | solution.py:300
  284.0 183.7 %reduce-scatter.25.cloned.1.call-start = ((), (), s32[]{:S(2)}) async-start(), calls=%async_computation.22 | async-start | bytes 1572864 | tf_op jit(solution)/shard_map/reduce_scatter | solution.py:302
  352.4 115.4 %reduce-scatter.29.cloned.1.call-start = ((), (), s32[]{:S(2)}) async-start(), calls=%async_computation.24 | async-start | bytes 3145728 | tf_op jit(solution)/shard_map/reduce_scatter | solution.py:304
  370.2 97.6 %reduce-scatter.27.cloned.1.call-start = ((), (), s32[]{:S(2)}) async-start(), calls=%async_computation.23 | async-start | bytes 3145728 | tf_op jit(solution)/shard_map/reduce_scatter | solution.py:303
  371.4 28.0 %collective-permute-start.4 = (bf16[16,1024]{1,0:T(8,128)(2,1)S(1)}, bf16[16,1024]{1,0:T(8,128)(2,1)S(1)}, u32[]{:S(2)}, u32[]{:S(2)}) collective-permute-start(bf16[16,1024]{1,0:T(8,128)(2,1)S(1)} %get-tuple-element.396), channel_id=1, source_target_pairs={{2,0},{4,2},{6,4},{8,6},{10,8},{12,10},{14,12},{16,14},{18,16},{20... | collective-permute-start | bytes 98312 | tf_op jit(solution)/shard_map/ppermute | solution.py:24
  372.7 26.8 %collective-permute-start.5 = (bf16[16,1024]{1,0:T(8,128)(2,1)S(1)}, bf16[16,1024]{1,0:T(8,128)(2,1)S(1)}, u32[]{:S(2)}, u32[]{:S(2)}) collective-permute-start(bf16[16,1024]{1,0:T(8,128)(2,1)S(1)} %get-tuple-element.397), channel_id=1, source_target_pairs={{0,2},{2,4},{4,6},{6,8},{8,10},{10,12},{12,14},{14,16},{16,18},{18... | collective-permute-start | bytes 98312 | tf_op jit(solution)/shard_map/ppermute | solution.py:21
  376.4 12.5 %collective-permute-start.6 = (bf16[16,1024]{1,0:T(8,128)(2,1)}, bf16[16,1024]{1,0:T(8,128)(2,1)S(1)}, u32[]{:S(2)}, u32[]{:S(2)}) collective-permute-start(bf16[16,1024]{1,0:T(8,128)(2,1)} %get-tuple-element.400), channel_id=1, source_target_pairs={{2,0},{4,2},{6,4},{8,6},{10,8},{12,10},{14,12},{16,14},{18,16},{20... | collective-permute-start | bytes 98312 | tf_op jit(solution)/shard_map/ppermute | solution.py:24
  377.7 11.2 %collective-permute-start.7 = (bf16[16,1024]{1,0:T(8,128)(2,1)S(1)}, bf16[16,1024]{1,0:T(8,128)(2,1)S(1)}, u32[]{:S(2)}, u32[]{:S(2)}) collective-permute-start(bf16[16,1024]{1,0:T(8,128)(2,1)S(1)} %get-tuple-element.401), channel_id=1, source_target_pairs={{0,2},{2,4},{4,6},{6,8},{8,10},{10,12},{12,14},{14,16},{16,18},{18... | collective-permute-start | bytes 98312 | tf_op jit(solution)/shard_map/ppermute | solution.py:21
  382.5 99.8 %reduce-scatter.15.cloned.1.call-start = ((), (), s32[]{:S(2)}) async-start(), calls=%async_computation.17 | async-start | bytes 3145728 | tf_op jit(solution)/shard_map/reduce_scatter | solution.py:297
  443.5 73.3 %reduce-scatter.13.cloned.1.call-start = ((), (), s32[]{:S(2)}) async-start(), calls=%async_computation.16 | async-start | bytes 3145728 | tf_op jit(solution)/shard_map/reduce_scatter | solution.py:296
  451.0 145.7 %reduce-scatter.17.cloned.1.call-start = ((), (), s32[]{:S(2)}) async-start(), calls=%async_computation.18 | async-start | bytes 9437184 | tf_op jit(solution)/shard_map/reduce_scatter | solution.py:298
  467.3 322.7 %all-reduce.6.cloned.1.call-start = ((), (), s32[]{:S(2)}) async-start(), calls=%async_computation.25 | async-start | bytes 18874368 | tf_op jit(solution)/shard_map/psum | solution.py:306
  (85 other events, 958.5 us)
Sparse Core Ops, SparseCore 0:
  10.1 30.0 all-gather.11
  42.4 26.1 all-gather.9
  70.7 45.4 all-gather.13
  118.2 21.2 all-gather.17
  141.5 22.1 all-gather.15
  278.2 8.4 reduce-scatter.10
  289.5 20.2 reduce-scatter.22
  312.8 20.3 reduce-scatter.18
  335.9 20.3 reduce-scatter.20
  359.1 20.3 reduce-scatter.24
  381.6 31.8 reduce-scatter.28
  415.7 31.8 reduce-scatter.26
  450.4 31.8 reduce-scatter.14
  485.0 31.8 reduce-scatter.12
  519.6 77.0 reduce-scatter.16
  602.0 187.9 all-reduce.5
